TPU v7x, 512 devices: a whole 4x8x8 slice. The times are simulated.
512 devices in a mesh: dp: 16 (over z, core), seq: 32 (over x, y).
Axes of the slice: x: 4, y: 8, z: 8, core: 2. Of those that a mesh axis runs over, the one named last changes fastest.
Arguments:
- queries: bfloat16 [65536, 4096], P(('dp', 'seq')), may hold values from -6 to 6
- keys: bfloat16 [65536, 512], P(('dp', 'seq')), may hold values from -6 to 6
- values: bfloat16 [65536, 512], P(('dp', 'seq')), may hold values from -6 to 6
- d_out: bfloat16 [65536, 4096], P(('dp', 'seq')), may hold values from -6 to 6
- doc_lengths: int32 [171], replicated, may hold values from 1 to 768, as said below
Outputs:
- d_queries: bfloat16 [65536, 4096], P(('dp', 'seq'))
- key_gradient: bfloat16 [65536, 512], P(('dp', 'seq'))
- value_gradient: bfloat16 [65536, 512], P(('dp', 'seq'))
Inputs may be any that keep to these rules, and one draw needn't show every extreme that they name: `doc_lengths`: lengths of the 171 documents in order; they sum to 65536, and the longest has exactly 768 tokens.
All inputs are finite; a program needn't handle non-finite values.
Results may differ from a plain program's by a relative error of at most 0.008.
Values may be sent and summed in bfloat16 or wider, within the bound.
A program may use at most 64 MiB of HBM per device.

v0:
```python
import math
import jax
import jax.numpy as jnp
from jax import lax
from jax.sharding import PartitionSpec as P

HEAD_SIZE = 128
GROUP = 8
DOC_MOST = 768


def from_behind(value, axis, steps):
    count = lax.axis_size(axis)
    leading, last = (max(0, -steps), min(count, count - steps))
    return lax.ppermute(value, axis, [(source, source + steps) for source in range(leading, last)])


def as_sent(shard):
    return jax.tree.map(lambda a: a.astype(jnp.bfloat16) if a.dtype == jnp.float32 else a, shard)


def doc_index(positions, doc_ends):
    return jnp.sum((positions[:, None] >= doc_ends[None, :]).astype(jnp.int32), axis=1)


def block_grads(q_rows, key_rows, value_rows, grad_rows, allowed, score_scale):
    scores = jnp.dot(q_rows, key_rows.T, preferred_element_type=jnp.float32) * score_scale
    scores = jnp.where(allowed, scores, -1e30)
    row_max = jnp.max(scores, axis=1, keepdims=True)
    exp_scores = jnp.exp(scores - row_max)
    attn_probs = exp_scores / jnp.sum(exp_scores, axis=1, keepdims=True)
    probs_low = attn_probs.astype(jnp.bfloat16)
    grad_probs = jnp.dot(grad_rows, value_rows.T, preferred_element_type=jnp.float32)
    row_delta = jnp.sum(attn_probs * grad_probs, axis=1, keepdims=True)
    grad_scores = (attn_probs * (grad_probs - row_delta) * score_scale).astype(jnp.bfloat16)
    grad_q = jnp.dot(grad_scores, key_rows, preferred_element_type=jnp.float32)
    grad_k = jnp.dot(grad_scores.T, q_rows, preferred_element_type=jnp.float32)
    grad_v = jnp.dot(probs_low.T, grad_rows, preferred_element_type=jnp.float32)
    return (grad_q, grad_k, grad_v)


def local(queries, keys, values, d_out, doc_lengths):
    tok_rows, q_width = queries.shape
    seq_devices = lax.axis_size("seq")
    kv_width = keys.shape[1]
    kv_heads = kv_width // HEAD_SIZE
    doc_ends = jnp.cumsum(doc_lengths)
    score_scale = 1.0 / math.sqrt(HEAD_SIZE)
    block_rows = tok_rows * seq_devices
    spread_k = jnp.broadcast_to(
        keys.reshape(tok_rows, kv_heads, 1, HEAD_SIZE), (tok_rows, kv_heads, GROUP, HEAD_SIZE)
    ).reshape(tok_rows, q_width)
    spread_v = jnp.broadcast_to(
        values.reshape(tok_rows, kv_heads, 1, HEAD_SIZE), (tok_rows, kv_heads, GROUP, HEAD_SIZE)
    ).reshape(tok_rows, q_width)
    head_q, head_g, head_k, head_v = (
        lax.all_to_all(queries, "seq", split_axis=1, concat_axis=0, tiled=True),
        lax.all_to_all(d_out, "seq", split_axis=1, concat_axis=0, tiled=True),
        lax.all_to_all(spread_k, "seq", split_axis=1, concat_axis=0, tiled=True),
        lax.all_to_all(spread_v, "seq", split_axis=1, concat_axis=0, tiled=True),
    )
    tail_pair = jnp.stack([head_k, head_v])
    prior_pair = from_behind(tail_pair, "dp", 1)
    all_k = jnp.concatenate([prior_pair[0], head_k], axis=0)
    all_v = jnp.concatenate([prior_pair[1], head_v], axis=0)
    block_start = lax.axis_index("dp") * block_rows
    query_span = min(512, block_rows)
    key_window = query_span + DOC_MOST
    steps_count = block_rows // query_span
    query_pos = block_start + jnp.arange(block_rows, dtype=jnp.int32)
    key_pos = block_start - block_rows + jnp.arange(block_rows + block_rows, dtype=jnp.int32)
    query_docs = doc_index(query_pos, doc_ends)
    key_docs = doc_index(key_pos, doc_ends)

    def step(totals, step_index):
        acc_k, acc_v = totals
        row_start = step_index * query_span
        key_start = row_start + block_rows - DOC_MOST
        q_rows = lax.dynamic_slice_in_dim(head_q, row_start, query_span, 0)
        g_rows = lax.dynamic_slice_in_dim(head_g, row_start, query_span, 0)
        key_rows = lax.dynamic_slice_in_dim(all_k, key_start, key_window, 0)
        value_rows = lax.dynamic_slice_in_dim(all_v, key_start, key_window, 0)
        q_pos = lax.dynamic_slice_in_dim(query_pos, row_start, query_span, 0)
        k_pos = lax.dynamic_slice_in_dim(key_pos, key_start, key_window, 0)
        q_docs = lax.dynamic_slice_in_dim(query_docs, row_start, query_span, 0)
        k_docs = lax.dynamic_slice_in_dim(key_docs, key_start, key_window, 0)
        allowed = (
            (q_docs[:, None] == k_docs[None, :])
            & (k_pos[None, :] <= q_pos[:, None])
            & (k_pos[None, :] >= 0)
        )
        grad_q, grad_k, grad_v = block_grads(
            q_rows, key_rows, value_rows, g_rows, allowed, score_scale
        )
        acc_k = lax.dynamic_update_slice_in_dim(
            acc_k, lax.dynamic_slice_in_dim(acc_k, key_start, key_window, 0) + grad_k, key_start, 0
        )
        acc_v = lax.dynamic_update_slice_in_dim(
            acc_v, lax.dynamic_slice_in_dim(acc_v, key_start, key_window, 0) + grad_v, key_start, 0
        )
        return ((acc_k, acc_v), grad_q.astype(jnp.bfloat16))

    empty_acc = jnp.zeros((block_rows + block_rows, HEAD_SIZE), jnp.float32)
    (acc_k, acc_v), q_blocks = lax.scan(
        step, (empty_acc, empty_acc), jnp.arange(steps_count, dtype=jnp.int32)
    )
    grads_q = q_blocks.reshape(block_rows, HEAD_SIZE)
    back_pair = from_behind(
        jnp.stack([acc_k[:block_rows], acc_v[:block_rows]]).astype(jnp.bfloat16), "dp", -1
    ).astype(jnp.float32)
    own_k = acc_k[block_rows:]
    own_v = acc_v[block_rows:]
    split_at = block_rows - block_rows
    term_k = jnp.concatenate([own_k[:split_at], own_k + back_pair[0]], axis=0)
    term_v = jnp.concatenate([own_v[:split_at], own_v + back_pair[1]], axis=0)
    tok_dq = lax.all_to_all(grads_q, "seq", split_axis=0, concat_axis=1, tiled=True)
    tok_k, tok_v = (
        lax.all_to_all(as_sent(term_k), "seq", split_axis=0, concat_axis=1, tiled=True).astype(
            term_k.dtype
        ),
        lax.all_to_all(as_sent(term_v), "seq", split_axis=0, concat_axis=1, tiled=True).astype(
            term_v.dtype
        ),
    )
    key_gradient = (
        jnp.sum(tok_k.reshape(tok_rows, kv_heads, GROUP, HEAD_SIZE), axis=2)
        .reshape(tok_rows, kv_width)
        .astype(jnp.bfloat16)
    )
    value_gradient = (
        jnp.sum(tok_v.reshape(tok_rows, kv_heads, GROUP, HEAD_SIZE), axis=2)
        .reshape(tok_rows, kv_width)
        .astype(jnp.bfloat16)
    )
    return (tok_dq, key_gradient, value_gradient)


def solution(mesh):
    in_specs = (
        P(("dp", "seq"), None),
        P(("dp", "seq"), None),
        P(("dp", "seq"), None),
        P(("dp", "seq"), None),
        P(),
    )
    out_specs = (P(("dp", "seq"), None), P(("dp", "seq"), None), P(("dp", "seq"), None))
    return jax.shard_map(local, mesh=mesh, in_specs=in_specs, out_specs=out_specs, check_vma=False)
```

profile of v0, /device:TPU:448, one launch (start us, length us, event | category | flops | bytes accessed | tf_op | source)
XLA Modules:
  0.0 370.4 jit_solution(15627165320955770170)
XLA Ops:
  2.9 10.0 %all-to-all-start.2 = ((bf16[128,32,128]{2,0,1:T(8,128)(2,1)}), bf16[128,32,128]{2,0,1:T(8,128)(2,1)S(1)}, u32[]{:S(2)}, u32[]{:S(2)}) async-start(bf16[128,32,128]{2,0,1:T(8,128)(2,1)} %bitcast.9), calls=%async_computation.2 | async-start | bytes 2097152 | tf_op jit(solution)/shard_map/all_to_all | solution.py:60
  12.9 28.6 %all-to-all-done.2 = bf16[128,32,128]{2,0,1:T(8,128)(2,1)S(1)} async-done(((bf16[128,32,128]{2,0,1:T(8,128)(2,1)}), bf16[128,32,128]{2,0,1:T(8,128)(2,1)S(1)}, u32[]{:S(2)}, u32[]{:S(2)}) %all-to-all-start.2) | async-done | bytes 1048608 | tf_op jit(solution)/shard_map/all_to_all | solution.py:60
  42.7 5.1 %all-to-all-start.1 = ((bf16[128,32,128]{2,0,1:T(8,128)(2,1)}), bf16[128,32,128]{2,0,1:T(8,128)(2,1)S(1)}, u32[]{:S(2)}, u32[]{:S(2)}) async-start(bf16[128,32,128]{2,0,1:T(8,128)(2,1)} %bitcast.99), calls=%async_computation.1 | async-start | bytes 2097152 | tf_op jit(solution)/shard_map/all_to_all | solution.py:59
  49.1 27.0 %all-to-all-done.1 = bf16[128,32,128]{2,0,1:T(8,128)(2,1)S(1)} async-done(((bf16[128,32,128]{2,0,1:T(8,128)(2,1)}), bf16[128,32,128]{2,0,1:T(8,128)(2,1)S(1)}, u32[]{:S(2)}, u32[]{:S(2)}) %all-to-all-start.1) | async-done | bytes 1048608 | tf_op jit(solution)/shard_map/all_to_all | solution.py:59
  76.1 5.0 %all-to-all-start = ((bf16[128,32,128]{2,0,1:T(8,128)(2,1)}), bf16[128,32,128]{2,0,1:T(8,128)(2,1)}, u32[]{:S(2)}, u32[]{:S(2)}) async-start(bf16[128,32,128]{2,0,1:T(8,128)(2,1)} %copy_bitcast_fusion.1), calls=%async_computation | async-start | bytes 2097152 | tf_op jit(solution)/shard_map/all_to_all | solution.py:57
  88.5 21.0 %all-to-all-done = bf16[128,32,128]{2,0,1:T(8,128)(2,1)} async-done(((bf16[128,32,128]{2,0,1:T(8,128)(2,1)}), bf16[128,32,128]{2,0,1:T(8,128)(2,1)}, u32[]{:S(2)}, u32[]{:S(2)}) %all-to-all-start) | async-done | bytes 1048608 | tf_op jit(solution)/shard_map/all_to_all | solution.py:57
  109.4 5.0 %all-to-all-start.3 = ((bf16[128,32,128]{2,0,1:T(8,128)(2,1)}), bf16[128,32,128]{2,0,1:T(8,128)(2,1)}, u32[]{:S(2)}, u32[]{:S(2)}) async-start(bf16[128,32,128]{2,0,1:T(8,128)(2,1)} %copy_bitcast_fusion), calls=%async_computation.3 | async-start | bytes 2097152 | tf_op jit(solution)/shard_map/all_to_all | solution.py:58
  118.8 23.9 %all-to-all-done.3 = bf16[128,32,128]{2,0,1:T(8,128)(2,1)} async-done(((bf16[128,32,128]{2,0,1:T(8,128)(2,1)}), bf16[128,32,128]{2,0,1:T(8,128)(2,1)}, u32[]{:S(2)}, u32[]{:S(2)}) %all-to-all-start.3) | async-done | bytes 1048608 | tf_op jit(solution)/shard_map/all_to_all | solution.py:58
  147.2 113.3 %while.18 = (s32[]{:T(128)}, f32[8192,128]{1,0:T(8,128)}, f32[8192,128]{1,0:T(8,128)}, bf16[8,512,128]{2,1,0:T(8,128)(2,1)}, s32[8]{0:T(128)S(1)}, /*index=5*/s3...) while((s32[]{:T(128)}, f32[8192,128]{1,0:T(8,128)}, ...), condition=%wide.region_8.9_spmd, body=%wide.region_4.0_spmd.sunk | while | flops 853671680 | bytes 26610516 | solution.py:104
  156.0 2.8 fusion.55
  170.2 2.8 fusion.55
  184.4 2.8 fusion.55
  198.5 2.8 fusion.55
  212.7 2.8 fusion.55
  226.9 2.8 fusion.55
  241.0 2.8 fusion.55
  255.2 2.8 fusion.55
  267.4 4.9 %all-to-all-start.4 = ((bf16[32,128,128]{2,1,0:T(8,128)(2,1)}), bf16[32,128,128]{2,1,0:T(8,128)(2,1)S(1)}, u32[]{:S(2)}, u32[]{:S(2)}) async-start(bf16[32,128,128]{2,1,0:T(8,128)(2,1)} %bitcast.18), calls=%async_computation.4 | async-start | bytes 2097152 | tf_op jit(solution)/shard_map/all_to_all | solution.py:116
  272.3 18.9 %collective-permute-done.1 = bf16[2,4096,128]{2,1,0:T(8,128)(2,1)} collective-permute-done((bf16[2,4096,128]{2,1,0:T(8,128)(2,1)}, bf16[2,4096,128]{2,1,0:T(8,128)(2,1)}, u32[]{:S(2)}, u32[]{:S(2)}) %collective-permute-start.1) | collective-permute-done | bytes 2097184 | tf_op jit(solution)/shard_map/ppermute | solution.py:15
  293.1 3.2 fusion.23
  296.3 3.9 %all-to-all-done.4 = bf16[32,128,128]{2,1,0:T(8,128)(2,1)S(1)} async-done(((bf16[32,128,128]{2,1,0:T(8,128)(2,1)}), bf16[32,128,128]{2,1,0:T(8,128)(2,1)S(1)}, u32[]{:S(2)}, u32[]{:S(2)}) %all-to-all-start.4) | async-done | bytes 1048608 | tf_op jit(solution)/shard_map/all_to_all | solution.py:116
  300.2 35.8 %all_to_all.121 = bf16[32,128,128]{2,1,0:T(8,128)(2,1)} all-to-all(bf16[32,128,128]{2,1,0:T(8,128)(2,1)S(1)} %bitcast.98), channel_id=1, replica_groups=mesh['dp'=16,'seq'=32] {'seq'}, dimensions={0} | all-to-all | bytes 2097152 | tf_op jit(solution)/shard_map/all_to_all | solution.py:118
  336.0 5.1 %all-to-all-start.6 = ((bf16[32,128,128]{2,1,0:T(8,128)(2,1)}), bf16[32,128,128]{2,1,0:T(8,128)(2,1)S(1)}, u32[]{:S(2)}, u32[]{:S(2)}) async-start(bf16[32,128,128]{2,1,0:T(8,128)(2,1)} %bitcast.29), calls=%async_computation.6 | async-start | bytes 2097152 | tf_op jit(solution)/shard_map/all_to_all | solution.py:121
  345.9 23.5 %all-to-all-done.6 = bf16[32,128,128]{2,1,0:T(8,128)(2,1)S(1)} async-done(((bf16[32,128,128]{2,1,0:T(8,128)(2,1)}), bf16[32,128,128]{2,1,0:T(8,128)(2,1)S(1)}, u32[]{:S(2)}, u32[]{:S(2)}) %all-to-all-start.6) | async-done | bytes 1048608 | tf_op jit(solution)/shard_map/all_to_all | solution.py:121
  (136 shorter events, 120.9 us)
Async XLA Ops:
  0.6 47.2 %copy-start = (bf16[128,4096]{1,0:T(8,128)(2,1)S(1)}, bf16[128,4096]{1,0:T(8,128)(2,1)}, u32[]{:S(2)}) copy-start(bf16[128,4096]{1,0:T(8,128)(2,1)} %param.7) | copy-start | bytes 3145732
  0.6 12.2 %copy-start.3 = (bf16[128,512]{1,0:T(8,128)(2,1)S(1)}, bf16[128,512]{1,0:T(8,128)(2,1)}, u32[]{:S(2)}) copy-start(bf16[128,512]{1,0:T(8,128)(2,1)} %param.8) | copy-start | bytes 393220
  2.9 38.6 %all-to-all-start.2 = ((bf16[128,32,128]{2,0,1:T(8,128)(2,1)}), bf16[128,32,128]{2,0,1:T(8,128)(2,1)S(1)}, u32[]{:S(2)}, u32[]{:S(2)}) async-start(bf16[128,32,128]{2,0,1:T(8,128)(2,1)} %bitcast.9), calls=%async_computation.2 | async-start | bytes 2097152 | tf_op jit(solution)/shard_map/all_to_all | solution.py:60
  42.7 33.4 %all-to-all-start.1 = ((bf16[128,32,128]{2,0,1:T(8,128)(2,1)}), bf16[128,32,128]{2,0,1:T(8,128)(2,1)S(1)}, u32[]{:S(2)}, u32[]{:S(2)}) async-start(bf16[128,32,128]{2,0,1:T(8,128)(2,1)} %bitcast.99), calls=%async_computation.1 | async-start | bytes 2097152 | tf_op jit(solution)/shard_map/all_to_all | solution.py:59
  76.1 33.3 %all-to-all-start = ((bf16[128,32,128]{2,0,1:T(8,128)(2,1)}), bf16[128,32,128]{2,0,1:T(8,128)(2,1)}, u32[]{:S(2)}, u32[]{:S(2)}) async-start(bf16[128,32,128]{2,0,1:T(8,128)(2,1)} %copy_bitcast_fusion.1), calls=%async_computation | async-start | bytes 2097152 | tf_op jit(solution)/shard_map/all_to_all | solution.py:57
  81.1 3.5 copy-start.4
  82.7 32.2 %collective-permute-start = (bf16[2,4096,128]{2,1,0:T(8,128)(2,1)}, bf16[2,4096,128]{2,1,0:T(8,128)(2,1)}, u32[]{:S(2)}, u32[]{:S(2)}) collective-permute-start(bf16[2,4096,128]{2,1,0:T(8,128)(2,1)} %pad_maximum_fusion), channel_id=1, source_target_pairs={{0,32},{32,64},{64,96},{96,128},{128,160},{160,192},{192,224},{224... | collective-permute-start | bytes 6291464 | tf_op jit(solution)/shard_map/ppermute | solution.py:15
  109.4 33.3 %all-to-all-start.3 = ((bf16[128,32,128]{2,0,1:T(8,128)(2,1)}), bf16[128,32,128]{2,0,1:T(8,128)(2,1)}, u32[]{:S(2)}, u32[]{:S(2)}) async-start(bf16[128,32,128]{2,0,1:T(8,128)(2,1)} %copy_bitcast_fusion), calls=%async_computation.3 | async-start | bytes 2097152 | tf_op jit(solution)/shard_map/all_to_all | solution.py:58
  265.5 25.8 %collective-permute-start.1 = (bf16[2,4096,128]{2,1,0:T(8,128)(2,1)}, bf16[2,4096,128]{2,1,0:T(8,128)(2,1)}, u32[]{:S(2)}, u32[]{:S(2)}) collective-permute-start(bf16[2,4096,128]{2,1,0:T(8,128)(2,1)} %pad_maximum_fusion.3), channel_id=1, source_target_pairs={{32,0},{64,32},{96,64},{128,96},{160,128},{192,160},{224,192},{256... | collective-permute-start | bytes 6291464 | tf_op jit(solution)/shard_map/ppermute | solution.py:15
  267.4 32.8 %all-to-all-start.4 = ((bf16[32,128,128]{2,1,0:T(8,128)(2,1)}), bf16[32,128,128]{2,1,0:T(8,128)(2,1)S(1)}, u32[]{:S(2)}, u32[]{:S(2)}) async-start(bf16[32,128,128]{2,1,0:T(8,128)(2,1)} %bitcast.18), calls=%async_computation.4 | async-start | bytes 2097152 | tf_op jit(solution)/shard_map/all_to_all | solution.py:116
  272.3 20.8 %copy-start.1 = (f32[8192,128]{1,0:T(8,128)S(1)}, f32[8192,128]{1,0:T(8,128)}, u32[]{:S(2)}) copy-start(f32[8192,128]{1,0:T(8,128)} %get-tuple-element.261) | copy-start | bytes 12582916
  336.0 33.4 %all-to-all-start.6 = ((bf16[32,128,128]{2,1,0:T(8,128)(2,1)}), bf16[32,128,128]{2,1,0:T(8,128)(2,1)S(1)}, u32[]{:S(2)}, u32[]{:S(2)}) async-start(bf16[32,128,128]{2,1,0:T(8,128)(2,1)} %bitcast.29), calls=%async_computation.6 | async-start | bytes 2097152 | tf_op jit(solution)/shard_map/all_to_all | solution.py:121
  342.5 2.4 copy-start.2
where the time goes:
time: 373 us; the launch traced here: 370 us
  waiting for transfers between devices  147 us (39%)
  matrix products  90.5 us (24%)
  starting transfers between devices  38.9 us (10%)
  blocking collectives  35.8 us (10%)
  local copies, waits for them, and re-layouts  29 us (8%)
  other arithmetic  23.1 us (6%)
  loops' own time  5.39 us (1%)
    all_to_all x1, blocking collectives, local(): lax.all_to_all(as_sent(term_k), 'seq', split_axis=0, concat_axis=1, tiled...  35.8 us
    all_to_all x1, waiting for transfers between devices, local(): lax.all_to_all(spread_v, 'seq', split_axis=1, concat_axis=0, tiled=True)  28.6 us
    all_to_all x1, waiting for transfers between devices, local(): lax.all_to_all(spread_k, 'seq', split_axis=1, concat_axis=0, tiled=True)  27 us
    all_to_all x1, waiting for transfers between devices, local(): lax.all_to_all(d_out, 'seq', split_axis=1, concat_axis=0, tiled=True)  23.9 us
    all_to_all x1, waiting for transfers between devices, local(): lax.all_to_all(as_sent(term_v), 'seq', split_axis=0, concat_axis=1, tiled...  23.5 us
    dot_general x8, matrix products, block_grads(): grad_v = jnp.dot(probs_low.T, grad_rows, preferred_element_type=jnp.float32)  22.3 us
    all_to_all x1, waiting for transfers between devices, local(): lax.all_to_all(queries, 'seq', split_axis=1, concat_axis=0, tiled=True)  21 us
    dot_general x8, matrix products, block_grads(): grad_k = jnp.dot(grad_scores.T, q_rows, preferred_element_type=jnp.float32)  20.4 us
  transfers between devices with their start and end apart: 8, of which 7 were waited for; matrix products, arithmetic and copies ran while one was open for 6% of the time, Pallas kernels for 0%

commit v1 on v0

--- a/solution.py
+++ b/solution.py
@@ -57,7 +57,12 @@
         lax.all_to_all(queries, "seq", split_axis=1, concat_axis=0, tiled=True),
         lax.all_to_all(d_out, "seq", split_axis=1, concat_axis=0, tiled=True),
         lax.all_to_all(spread_k, "seq", split_axis=1, concat_axis=0, tiled=True),
-        lax.all_to_all(spread_v, "seq", split_axis=1, concat_axis=0, tiled=True),
+        jnp.concatenate(
+            lax.all_to_all(
+                jnp.stack(jnp.split(spread_v, lax.axis_size("seq"), axis=1)), "seq", 0, 0
+            ),
+            axis=0,
+        ),
     )
     tail_pair = jnp.stack([head_k, head_v])
     prior_pair = from_behind(tail_pair, "dp", 1)

time: 373 us -> 371 us (level)
    all_to_all x1, starting transfers between devices: 5.07 us -> 9.95 us  [local(): lax.all_to_all(spread_k, 'seq', split_axis=1, concat_axis=0, tiled=True)]
    all_to_all x1, starting transfers between devices: 9.95 us -> 5.07 us  [local(): lax.all_to_all(jnp.stack(jnp.split(spread_v, lax.axis_size('seq'), axis=1...]
where the time goes in v1:
time: 371 us; the launch traced here: 369 us
  waiting for transfers between devices  144 us (39%)
  matrix products  90.5 us (24%)
  starting transfers between devices  39 us (11%)
  blocking collectives  35.8 us (10%)
  local copies, waits for them, and re-layouts  30 us (8%)
  other arithmetic  23.1 us (6%)
  loops' own time  5.39 us (1%)
    all_to_all x1, blocking collectives, local(): lax.all_to_all(as_sent(term_k), 'seq', split_axis=0, concat_axis=1, tiled...  35.8 us
    all_to_all x1, waiting for transfers between devices, local(): lax.all_to_all(jnp.stack(jnp.split(spread_v, lax.axis_size('seq'), axis=1...  27 us
    all_to_all x1, waiting for transfers between devices, local(): lax.all_to_all(spread_k, 'seq', split_axis=1, concat_axis=0, tiled=True)  26.2 us
    all_to_all x1, waiting for transfers between devices, local(): lax.all_to_all(d_out, 'seq', split_axis=1, concat_axis=0, tiled=True)  23.9 us
    all_to_all x1, waiting for transfers between devices, local(): lax.all_to_all(as_sent(term_v), 'seq', split_axis=0, concat_axis=1, tiled...  23.5 us
    dot_general x8, matrix products, block_grads(): grad_v = jnp.dot(probs_low.T, grad_rows, preferred_element_type=jnp.float32)  22.3 us
    all_to_all x1, waiting for transfers between devices, local(): lax.all_to_all(queries, 'seq', split_axis=1, concat_axis=0, tiled=True)  21 us
    dot_general x8, matrix products, block_grads(): grad_k = jnp.dot(grad_scores.T, q_rows, preferred_element_type=jnp.float32)  20.4 us
  transfers between devices with their start and end apart: 8, of which 7 were waited for; matrix products, arithmetic and copies ran while one was open for 6% of the time, Pallas kernels for 0%

profile of v1, /device:TPU:448, one launch (start us, length us, event | category | flops | bytes accessed | tf_op | source)
XLA Modules:
  0.0 369.2 jit_solution(441683634494273779)
XLA Ops:
  2.9 10.0 %all-to-all-start.1 = ((bf16[128,32,128]{2,0,1:T(8,128)(2,1)}), bf16[128,32,128]{2,0,1:T(8,128)(2,1)S(1)}, u32[]{:S(2)}, u32[]{:S(2)}) async-start(bf16[128,32,128]{2,0,1:T(8,128)(2,1)} %bitcast.6), calls=%async_computation.1 | async-start | bytes 2097152 | tf_op jit(solution)/shard_map/all_to_all | solution.py:59
  15.3 26.2 %all-to-all-done.1 = bf16[128,32,128]{2,0,1:T(8,128)(2,1)S(1)} async-done(((bf16[128,32,128]{2,0,1:T(8,128)(2,1)}), bf16[128,32,128]{2,0,1:T(8,128)(2,1)S(1)}, u32[]{:S(2)}, u32[]{:S(2)}) %all-to-all-start.1) | async-done | bytes 1048608 | tf_op jit(solution)/shard_map/all_to_all | solution.py:59
  41.5 5.1 %all-to-all-start.2 = ((bf16[32,128,128]{2,1,0:T(8,128)(2,1)}), bf16[32,128,128]{2,1,0:T(8,128)(2,1)S(1)}, u32[]{:S(2)}, u32[]{:S(2)}) async-start(bf16[32,128,128]{2,1,0:T(8,128)(2,1)} %copy-done.3), calls=%async_computation.2 | async-start | bytes 2097152 | tf_op jit(solution)/shard_map/all_to_all | solution.py:61
  47.9 27.0 %all-to-all-done.2 = bf16[32,128,128]{2,1,0:T(8,128)(2,1)S(1)} async-done(((bf16[32,128,128]{2,1,0:T(8,128)(2,1)}), bf16[32,128,128]{2,1,0:T(8,128)(2,1)S(1)}, u32[]{:S(2)}, u32[]{:S(2)}) %all-to-all-start.2) | async-done | bytes 1048608 | tf_op jit(solution)/shard_map/all_to_all | solution.py:61
  74.9 5.0 %all-to-all-start = ((bf16[128,32,128]{2,0,1:T(8,128)(2,1)}), bf16[128,32,128]{2,0,1:T(8,128)(2,1)}, u32[]{:S(2)}, u32[]{:S(2)}) async-start(bf16[128,32,128]{2,0,1:T(8,128)(2,1)} %copy_bitcast_fusion.2), calls=%async_computation | async-start | bytes 2097152 | tf_op jit(solution)/shard_map/all_to_all | solution.py:57
  87.2 21.0 %all-to-all-done = bf16[128,32,128]{2,0,1:T(8,128)(2,1)} async-done(((bf16[128,32,128]{2,0,1:T(8,128)(2,1)}), bf16[128,32,128]{2,0,1:T(8,128)(2,1)}, u32[]{:S(2)}, u32[]{:S(2)}) %all-to-all-start) | async-done | bytes 1048608 | tf_op jit(solution)/shard_map/all_to_all | solution.py:57
  108.2 5.0 %all-to-all-start.3 = ((bf16[128,32,128]{2,0,1:T(8,128)(2,1)}), bf16[128,32,128]{2,0,1:T(8,128)(2,1)}, u32[]{:S(2)}, u32[]{:S(2)}) async-start(bf16[128,32,128]{2,0,1:T(8,128)(2,1)} %copy_bitcast_fusion.1), calls=%async_computation.3 | async-start | bytes 2097152 | tf_op jit(solution)/shard_map/all_to_all | solution.py:58
  117.6 23.9 %all-to-all-done.3 = bf16[128,32,128]{2,0,1:T(8,128)(2,1)} async-done(((bf16[128,32,128]{2,0,1:T(8,128)(2,1)}), bf16[128,32,128]{2,0,1:T(8,128)(2,1)}, u32[]{:S(2)}, u32[]{:S(2)}) %all-to-all-start.3) | async-done | bytes 1048608 | tf_op jit(solution)/shard_map/all_to_all | solution.py:58
  146.0 113.3 %while.18 = (s32[]{:T(128)}, f32[8192,128]{1,0:T(8,128)}, f32[8192,128]{1,0:T(8,128)}, bf16[8,512,128]{2,1,0:T(8,128)(2,1)}, s32[8]{0:T(128)S(1)}, /*index=5*/s3...) while((s32[]{:T(128)}, f32[8192,128]{1,0:T(8,128)}, ...), condition=%wide.region_8.9_spmd, body=%wide.region_4.0_spmd.sunk | while | flops 853671680 | bytes 26610516 | solution.py:109
  154.8 2.8 fusion.54
  169.0 2.8 fusion.54
  183.1 2.8 fusion.54
  197.3 2.8 fusion.54
  211.5 2.8 fusion.54
  225.7 2.8 fusion.54
  239.8 2.8 fusion.54
  253.9 2.8 fusion.54
  266.2 4.9 %all-to-all-start.4 = ((bf16[32,128,128]{2,1,0:T(8,128)(2,1)}), bf16[32,128,128]{2,1,0:T(8,128)(2,1)S(1)}, u32[]{:S(2)}, u32[]{:S(2)}) async-start(bf16[32,128,128]{2,1,0:T(8,128)(2,1)} %bitcast.48), calls=%async_computation.4 | async-start | bytes 2097152 | tf_op jit(solution)/shard_map/all_to_all | solution.py:121
  271.1 18.9 %collective-permute-done.1 = bf16[2,4096,128]{2,1,0:T(8,128)(2,1)} collective-permute-done((bf16[2,4096,128]{2,1,0:T(8,128)(2,1)}, bf16[2,4096,128]{2,1,0:T(8,128)(2,1)}, u32[]{:S(2)}, u32[]{:S(2)}) %collective-permute-start.1) | collective-permute-done | bytes 2097184 | tf_op jit(solution)/shard_map/ppermute | solution.py:15
  291.9 3.2 fusion.23
  295.1 3.9 %all-to-all-done.4 = bf16[32,128,128]{2,1,0:T(8,128)(2,1)S(1)} async-done(((bf16[32,128,128]{2,1,0:T(8,128)(2,1)}), bf16[32,128,128]{2,1,0:T(8,128)(2,1)S(1)}, u32[]{:S(2)}, u32[]{:S(2)}) %all-to-all-start.4) | async-done | bytes 1048608 | tf_op jit(solution)/shard_map/all_to_all | solution.py:121
  299.0 35.8 %all_to_all.107 = bf16[32,128,128]{2,1,0:T(8,128)(2,1)} all-to-all(bf16[32,128,128]{2,1,0:T(8,128)(2,1)S(1)} %bitcast.254), channel_id=1, replica_groups=mesh['dp'=16,'seq'=32] {'seq'}, dimensions={0} | all-to-all | bytes 2097152 | tf_op jit(solution)/shard_map/all_to_all | solution.py:123
  334.8 5.1 %all-to-all-start.6 = ((bf16[32,128,128]{2,1,0:T(8,128)(2,1)}), bf16[32,128,128]{2,1,0:T(8,128)(2,1)S(1)}, u32[]{:S(2)}, u32[]{:S(2)}) async-start(bf16[32,128,128]{2,1,0:T(8,128)(2,1)} %bitcast.59), calls=%async_computation.6 | async-start | bytes 2097152 | tf_op jit(solution)/shard_map/all_to_all | solution.py:126
  344.7 23.5 %all-to-all-done.6 = bf16[32,128,128]{2,1,0:T(8,128)(2,1)S(1)} async-done(((bf16[32,128,128]{2,1,0:T(8,128)(2,1)}), bf16[32,128,128]{2,1,0:T(8,128)(2,1)S(1)}, u32[]{:S(2)}, u32[]{:S(2)}) %all-to-all-start.6) | async-done | bytes 1048608 | tf_op jit(solution)/shard_map/all_to_all | solution.py:126
  (171 shorter events, 121.9 us)
Async XLA Ops:
  0.6 46.0 %copy-start = (bf16[128,4096]{1,0:T(8,128)(2,1)S(1)}, bf16[128,4096]{1,0:T(8,128)(2,1)}, u32[]{:S(2)}) copy-start(bf16[128,4096]{1,0:T(8,128)(2,1)} %param.7) | copy-start | bytes 3145732
  0.6 12.2 %copy-start.4 = (bf16[128,512]{1,0:T(8,128)(2,1)S(1)}, bf16[128,512]{1,0:T(8,128)(2,1)}, u32[]{:S(2)}) copy-start(bf16[128,512]{1,0:T(8,128)(2,1)} %param.9) | copy-start | bytes 393220
  2.9 38.6 %all-to-all-start.1 = ((bf16[128,32,128]{2,0,1:T(8,128)(2,1)}), bf16[128,32,128]{2,0,1:T(8,128)(2,1)S(1)}, u32[]{:S(2)}, u32[]{:S(2)}) async-start(bf16[128,32,128]{2,0,1:T(8,128)(2,1)} %bitcast.6), calls=%async_computation.1 | async-start | bytes 2097152 | tf_op jit(solution)/shard_map/all_to_all | solution.py:59
  14.3 1.0 copy-start.3
  41.5 33.4 %all-to-all-start.2 = ((bf16[32,128,128]{2,1,0:T(8,128)(2,1)}), bf16[32,128,128]{2,1,0:T(8,128)(2,1)S(1)}, u32[]{:S(2)}, u32[]{:S(2)}) async-start(bf16[32,128,128]{2,1,0:T(8,128)(2,1)} %copy-done.3), calls=%async_computation.2 | async-start | bytes 2097152 | tf_op jit(solution)/shard_map/all_to_all | solution.py:61
  74.9 33.3 %all-to-all-start = ((bf16[128,32,128]{2,0,1:T(8,128)(2,1)}), bf16[128,32,128]{2,0,1:T(8,128)(2,1)}, u32[]{:S(2)}, u32[]{:S(2)}) async-start(bf16[128,32,128]{2,0,1:T(8,128)(2,1)} %copy_bitcast_fusion.2), calls=%async_computation | async-start | bytes 2097152 | tf_op jit(solution)/shard_map/all_to_all | solution.py:57
  79.9 3.5 copy-start.5
  81.5 32.2 %collective-permute-start = (bf16[2,4096,128]{2,1,0:T(8,128)(2,1)}, bf16[2,4096,128]{2,1,0:T(8,128)(2,1)}, u32[]{:S(2)}, u32[]{:S(2)}) collective-permute-start(bf16[2,4096,128]{2,1,0:T(8,128)(2,1)} %pad_maximum_fusion), channel_id=1, source_target_pairs={{0,32},{32,64},{64,96},{96,128},{128,160},{160,192},{192,224},{224... | collective-permute-start | bytes 6291464 | tf_op jit(solution)/shard_map/ppermute | solution.py:15
  108.2 33.3 %all-to-all-start.3 = ((bf16[128,32,128]{2,0,1:T(8,128)(2,1)}), bf16[128,32,128]{2,0,1:T(8,128)(2,1)}, u32[]{:S(2)}, u32[]{:S(2)}) async-start(bf16[128,32,128]{2,0,1:T(8,128)(2,1)} %copy_bitcast_fusion.1), calls=%async_computation.3 | async-start | bytes 2097152 | tf_op jit(solution)/shard_map/all_to_all | solution.py:58
  264.3 25.8 %collective-permute-start.1 = (bf16[2,4096,128]{2,1,0:T(8,128)(2,1)}, bf16[2,4096,128]{2,1,0:T(8,128)(2,1)}, u32[]{:S(2)}, u32[]{:S(2)}) collective-permute-start(bf16[2,4096,128]{2,1,0:T(8,128)(2,1)} %pad_maximum_fusion.3), channel_id=1, source_target_pairs={{32,0},{64,32},{96,64},{128,96},{160,128},{192,160},{224,192},{256... | collective-permute-start | bytes 6291464 | tf_op jit(solution)/shard_map/ppermute | solution.py:15
  266.2 32.8 %all-to-all-start.4 = ((bf16[32,128,128]{2,1,0:T(8,128)(2,1)}), bf16[32,128,128]{2,1,0:T(8,128)(2,1)S(1)}, u32[]{:S(2)}, u32[]{:S(2)}) async-start(bf16[32,128,128]{2,1,0:T(8,128)(2,1)} %bitcast.48), calls=%async_computation.4 | async-start | bytes 2097152 | tf_op jit(solution)/shard_map/all_to_all | solution.py:121
  271.1 20.8 %copy-start.1 = (f32[8192,128]{1,0:T(8,128)S(1)}, f32[8192,128]{1,0:T(8,128)}, u32[]{:S(2)}) copy-start(f32[8192,128]{1,0:T(8,128)} %get-tuple-element.261) | copy-start | bytes 12582916
  334.8 33.4 %all-to-all-start.6 = ((bf16[32,128,128]{2,1,0:T(8,128)(2,1)}), bf16[32,128,128]{2,1,0:T(8,128)(2,1)S(1)}, u32[]{:S(2)}, u32[]{:S(2)}) async-start(bf16[32,128,128]{2,1,0:T(8,128)(2,1)} %bitcast.59), calls=%async_computation.6 | async-start | bytes 2097152 | tf_op jit(solution)/shard_map/all_to_all | solution.py:126
  341.3 2.4 copy-start.2
